TPU v7x, 256 devices: a whole 4x4x8 slice. The times are simulated.
256 devices in a mesh: group: 8 (over x, core), expert: 32 (over y, z).
Axes of the slice: x: 4, y: 4, z: 8, core: 2. Of those that a mesh axis runs over, the one named last changes fastest.
Arguments:
- resid: bfloat16 [32768, 2048], P(('group', 'expert')), may hold values from -6 to 6
- queries: bfloat16 [32768, 2048], P(('group', 'expert')), may hold values from -48 to 48
- span_kv: bfloat16 [2, 32768, 2048], P(None, ('group', 'expert')), may hold values from -4 to 4
- cache_kv: bfloat16 [2, 256, 2, 128, 2048], P(None, ('group', 'expert')), may hold values from -6 to 6
- seg_len: int32 [256, 2], P(('group', 'expert')), may hold values from 0 to 128, as said below
- o_rows: bfloat16 [2048, 2048], P('expert'), may hold values from -0.125 to 0.125
- norm_gain: float32 [2048], replicated, may hold values from 0.25 to 1.75
- routes: int32 [32768, 8], P(('group', 'expert')), may hold values from 0 to 31, all different within a row; in each aligned block of 128 rows (0 to 127, 128 to 255, ...) at most 48 rows name the same one
- route_wts: float32 [32768, 8], P(('group', 'expert')), may hold values from 0.05 to 0.6
- w_in: bfloat16 [32, 2048, 1024], P('expert'), may hold values from -0.125 to 0.125
- w_out: bfloat16 [32, 512, 2048], P('expert'), may hold values from -0.25 to 0.25
Outputs:
- layer_out: bfloat16 [32768, 2048], P(('group', 'expert'))
Inputs may be any that keep to these rules, and one draw needn't show every extreme that they name: seg_len[d, 0] is 1 to 128; seg_len[d, 1] is 0 (the paired request is short) or 1 to 128; seg_len[0, 0] and seg_len[0, 1] are 128 and seg_len[1, 1] is 0. `routes`: each row names 8 different experts; among the 128 rows of one device no expert is named more than 48 times.
All inputs are finite; a program needn't handle non-finite values.
Results may differ from a plain program's by a relative error of at most 0.0053.
Values may be sent and summed in bfloat16 or wider, within the bound.
A program may use at most 128 MiB of HBM per device.

v0:
```python
import math

import jax
import jax.numpy as jnp
from jax import lax
from jax.sharding import PartitionSpec as P

HEADS = 16
HD = 128
FF = 512
TOPK = 8


def swapped(block, axis, distance):
    count = lax.axis_size(axis)
    route = []
    for low in range(count):
        high = low | 1 << distance
        if high != low and high < count:
            route += [(low, high), (high, low)]
    return lax.ppermute(block, axis, route)


def attend(query_rows, key_rows, value_rows, valid_keys):
    q_heads = query_rows.reshape(query_rows.shape[0], HEADS, HD)
    k_heads = key_rows.reshape(key_rows.shape[0], HEADS, HD)
    v_heads = value_rows.reshape(value_rows.shape[0], HEADS, HD)
    scores = jnp.einsum("chd,shd->hcs", q_heads, k_heads, preferred_element_type=jnp.float32) * (
        1.0 / math.sqrt(HD)
    )
    scores = jnp.where(valid_keys[None, None, :], scores, -1e30)
    peak_score = jnp.max(scores, axis=-1)
    expo = jnp.where(valid_keys[None, None, :], jnp.exp(scores - peak_score[..., None]), 0.0)
    totals = jnp.sum(expo, axis=-1)
    probs_low = expo.astype(jnp.bfloat16)
    accum_out = jnp.einsum("hcs,shd->chd", probs_low, v_heads, preferred_element_type=jnp.float32)
    return (peak_score, totals, accum_out)


def merge_parts(first, second):
    peak_a, total_a, accum_a = first
    peak_b, total_b, accum_b = second
    peak_both = jnp.maximum(peak_a, peak_b)
    scale_a = jnp.exp(peak_a - peak_both).T
    scale_b = jnp.exp(peak_b - peak_both).T
    numer = accum_a * scale_a[:, :, None] + accum_b * scale_b[:, :, None]
    denom = total_a.T * scale_a + total_b.T * scale_b
    merged = numer / denom[:, :, None]
    return merged.reshape(merged.shape[0], -1).astype(jnp.bfloat16)


def expert_mlp(token_rows, weight_in, weight_out):
    joined = jnp.dot(token_rows, weight_in, preferred_element_type=jnp.float32)
    hidden = (jax.nn.silu(joined[:, :FF]) * joined[:, FF:]).astype(jnp.bfloat16)
    return jnp.dot(hidden, weight_out, preferred_element_type=jnp.float32).astype(jnp.bfloat16)


def shards(
    resid, queries, span_kv, cache_kv, seg_len, o_rows, norm_gain, routes, route_wts, w_in, w_out
):
    span_rows = queries.shape[0]
    seg_rows = cache_kv.shape[3]
    width = queries.shape[1]
    experts_here = lax.axis_size("expert")
    positions = jnp.arange(seg_rows, dtype=jnp.int32)
    keys_a = jnp.concatenate([span_kv[0], cache_kv[0, 0, 0]], axis=0)
    vals_a = jnp.concatenate([span_kv[1], cache_kv[1, 0, 0]], axis=0)
    valid_a = jnp.concatenate([jnp.ones((span_rows,), bool), positions < seg_len[0, 0]])
    part_a = attend(queries, keys_a, vals_a, valid_a)
    length_low = seg_len[0, 1:2].astype(jnp.float32).astype(jnp.bfloat16)
    fetched, fetched_len = swapped((cache_kv[:, 0, 1], length_low), "group", 0)
    valid_b = positions.astype(jnp.float32) < fetched_len[0].astype(jnp.float32)
    part_b = attend(queries, fetched[0], fetched[1], valid_b)
    attended = merge_parts(part_a, part_b)
    projected = jnp.dot(
        attended,
        lax.all_gather(o_rows, "expert", axis=0, tiled=True),
        preferred_element_type=jnp.float32,
    )
    residual = resid.astype(jnp.float32) + projected
    normed = (
        residual
        * lax.rsqrt(jnp.mean(residual * residual, axis=-1, keepdims=True) + 1e-05)
        * norm_gain
    ).astype(jnp.bfloat16)
    capacity = min(span_rows, span_rows * TOPK * 3 // (2 * experts_here))
    onehot = (
        routes[:, :, None] == jnp.arange(experts_here, dtype=jnp.int32)[None, None, :]
    ).astype(jnp.int32)
    counts = jnp.sum(onehot, axis=1)
    before = jnp.cumsum(counts, axis=0) - counts
    slot_ids = jnp.sum(onehot * before[:, None, :], axis=-1)
    flat_slot = routes * capacity + slot_ids
    placing = jnp.any(
        flat_slot[None, :, :]
        == jnp.arange(experts_here * capacity, dtype=jnp.int32)[:, None, None],
        axis=-1,
    )
    outgoing = jnp.dot(
        placing.astype(jnp.bfloat16), normed, preferred_element_type=jnp.float32
    ).astype(jnp.bfloat16)
    outgoing = outgoing.reshape(experts_here, capacity, width)
    arrived = lax.all_to_all(outgoing, "expert", split_axis=0, concat_axis=0, tiled=True)
    flat_rows = arrived.reshape(-1, width)
    output_rows = expert_mlp(flat_rows, w_in[0], w_out[0]).reshape(arrived.shape)
    returned_rows = lax.all_to_all(output_rows, "expert", split_axis=0, concat_axis=0, tiled=True)
    returned_rows = returned_rows.reshape(experts_here * capacity, width)
    expert_sum = jnp.zeros((span_rows, width), jnp.float32)
    for route_k in range(TOPK):
        picked = returned_rows[flat_slot[:, route_k]].astype(jnp.float32)
        expert_sum = expert_sum + route_wts[:, route_k, None] * picked
    return (residual + expert_sum).astype(jnp.bfloat16)


def solution(mesh):
    placed = (
        P(("group", "expert"), None),
        P(("group", "expert"), None),
        P(None, ("group", "expert"), None),
        P(None, ("group", "expert"), None, None, None),
        P(("group", "expert"), None),
        P("expert", None),
        P(),
        P(("group", "expert"), None),
        P(("group", "expert"), None),
        P("expert", None, None),
        P("expert", None, None),
    )
    return jax.shard_map(
        shards, mesh=mesh, in_specs=placed, out_specs=P(("group", "expert"), None), check_vma=False
    )
```

profile of v0, /device:TPU:33, one launch (start us, length us, event | category | flops | bytes accessed | tf_op | source)
XLA Modules:
  0.0 480.1 jit_solution(5816244615594503621)
XLA Ops:
  6.5 0.7 all-gather.2.cloned.1.call-update
  7.3 1.3 fusion.66
  9.2 1.6 collective-permute-start
  10.8 1.3 slice.87
  12.1 1.3 copy.55
  13.4 0.0 collective-permute-start.1
  13.4 2.1 fusion.65
  15.5 1.3 copy.53
  16.8 1.1 copy.39
  17.9 2.3 fusion.63
  20.2 1.3 copy.54
  21.5 1.1 copy.40
  22.6 1.0 copy.35
  23.6 2.1 copy.36
  25.7 0.1 copy.47
  25.8 0.2 reduce_window_sum.11
  26.0 0.1 copy.49
  26.1 0.7 iota_compare_fusion.2
  26.8 5.6 %fusion = pred[1536,128]{1,0:T(8,128)(4,1)S(1)} fusion(s32[128,8]{0,1:T(8,128)S(1)} %multiply_add_fusion), kind=kLoop, calls=%fused_computation.11 | loop fusion | flops 2949120 | bytes 200704 | tf_op jit(solution)/shard_map/reduce_or | solution.py:94
  32.4 1.9 bitcast_reduce_fusion
  34.2 0.0 copy-start.1
  34.2 0.0 copy-start.3
  34.2 1.3 copy-done.1
  35.6 0.6 fusion.9
  37.0 0.0 collective-permute-done.1
  37.0 1.4 fusion.64
  38.4 0.5 fusion.67
  39.0 0.2 fusion.31
  39.2 0.8 fusion.14
  40.0 1.2 fusion.16
  41.2 67.7 %all-gather.2.cloned.1.call-done = bf16[2048,2048]{1,0:T(8,128)(2,1)} async-done(((bf16[64,2048]{1,0:T(8,128)(2,1)}), bf16[2048,2048]{1,0:T(8,128)(2,1)}) %all-gather.2.cloned.1.call-update) | async-done | bytes 8388624 | tf_op jit(solution)/shard_map/all_gather | solution.py:77
  108.9 4.9 %multiply_reduce_fusion = (f32[128]{0:T(128)S(1)}, f32[128,2048]{1,0:T(8,128)S(1)}) fusion(bf16[128,2048]{0,1:T(8,128)(2,1)} %bitcast.126, bf16[2048,2048]{1,0:T(8,128)(2,1)} %all-gather.2.cloned.1.call-done, bf16[128,2048]{1,0:T(8,128)(2,1)} %param.11), kind=kOutput, calls=%fused_computation.44 | convolution fusion | flops 1074790272 | bytes 10486272 | tf_op jit(solution)/shard_map/dot_general | solution.py:75
  113.9 1.9 convolution_convert_fusion.1
  115.8 0.0 copy-start.9
  115.8 146.3 %all_to_all.10 = bf16[32,48,2048]{2,1,0:T(8,128)(2,1)S(1)} all-to-all(bf16[32,48,2048]{2,1,0:T(8,128)(2,1)S(1)} %bitcast.120), channel_id=1, replica_groups=mesh['group'=8,'expert'=32] {'expert'}, dimensions={0} | all-to-all | bytes 12582912 | tf_op jit(solution)/shard_map/all_to_all | solution.py:103
  262.1 6.8 %fusion.1 = f32[1536,1024]{1,0:T(8,128)S(1)} fusion(bf16[1536,2048]{1,0:T(8,128)(2,1)S(1)} %bitcast.122, bf16[1,2048,1024]{2,1,0:T(8,128)(2,1)S(1)} %copy-done.9), kind=kOutput, calls=%fused_computation.12 | convolution fusion | flops 6442450944 | bytes 16777216 | tf_op jit(solution)/shard_map/dot_general | solution.py:53
  268.9 5.3 %convolution_convert_fusion = bf16[1536,2048]{1,0:T(8,128)(2,1)} fusion(bf16[1,512,2048]{2,1,0:T(8,128)(2,1)S(1)} %copy-done, f32[1536,1024]{1,0:T(8,128)S(1)} %fusion.1), kind=kOutput, calls=%fused_computation.8 | convolution fusion | flops 3229089792 | bytes 14680064 | tf_op jit(solution)/shard_map/dot_general | solution.py:55
  274.3 7.2 %all-to-all-start.1 = ((bf16[32,48,2048]{2,1,0:T(8,128)(2,1)}), bf16[32,48,2048]{2,1,0:T(8,128)(2,1)}, u32[]{:S(2)}, u32[]{:S(2)}) async-start(bf16[32,48,2048]{2,1,0:T(8,128)(2,1)} %bitcast.121), calls=%async_computation.1 | async-start | bytes 12582912 | tf_op jit(solution)/shard_map/all_to_all | solution.py:106
  281.6 140.6 %all-to-all-done.1 = bf16[32,48,2048]{2,1,0:T(8,128)(2,1)} async-done(((bf16[32,48,2048]{2,1,0:T(8,128)(2,1)}), bf16[32,48,2048]{2,1,0:T(8,128)(2,1)}, u32[]{:S(2)}, u32[]{:S(2)}) %all-to-all-start.1) | async-done | bytes 6291488 | tf_op jit(solution)/shard_map/all_to_all | solution.py:106
  422.2 5.8 %gather_fusion = bf16[128,2048]{1,0:T(8,128)(2,1)} fusion(bf16[1536,2048]{1,0:T(8,128)(2,1)} %bitcast.24, s32[1024]{0:T(1024)S(1)} %get-tuple-element.45), kind=kCustom, calls=%fused_computation | custom fusion | bytes 1049088 | tf_op jit(solution)/shard_map/gather | solution.py:110
  428.0 5.9 %gather_fusion.1 = bf16[128,2048]{1,0:T(8,128)(2,1)} fusion(bf16[1536,2048]{1,0:T(8,128)(2,1)} %bitcast.24, s32[1024]{0:T(1024)S(1)} %get-tuple-element.44), kind=kCustom, calls=%fused_computation.1 | custom fusion | bytes 1049088 | tf_op jit(solution)/shard_map/gather | solution.py:110
  433.9 5.9 %gather_fusion.2 = bf16[128,2048]{1,0:T(8,128)(2,1)} fusion(bf16[1536,2048]{1,0:T(8,128)(2,1)} %bitcast.24, s32[1024]{0:T(1024)S(1)} %get-tuple-element.43), kind=kCustom, calls=%fused_computation.2 | custom fusion | bytes 1049088 | tf_op jit(solution)/shard_map/gather | solution.py:110
  439.7 5.9 %gather_fusion.3 = bf16[128,2048]{1,0:T(8,128)(2,1)} fusion(bf16[1536,2048]{1,0:T(8,128)(2,1)} %bitcast.24, s32[1024]{0:T(1024)S(1)} %get-tuple-element.42), kind=kCustom, calls=%fused_computation.3 | custom fusion | bytes 1049088 | tf_op jit(solution)/shard_map/gather | solution.py:110
  445.6 5.8 %gather_fusion.4 = bf16[128,2048]{1,0:T(8,128)(2,1)} fusion(bf16[1536,2048]{1,0:T(8,128)(2,1)} %bitcast.24, s32[1024]{0:T(1024)S(1)} %get-tuple-element.41), kind=kCustom, calls=%fused_computation.4 | custom fusion | bytes 1049088 | tf_op jit(solution)/shard_map/gather | solution.py:110
  451.4 5.8 %gather_fusion.5 = bf16[128,2048]{1,0:T(8,128)(2,1)} fusion(bf16[1536,2048]{1,0:T(8,128)(2,1)} %bitcast.24, s32[1024]{0:T(1024)S(1)} %get-tuple-element.40), kind=kCustom, calls=%fused_computation.5 | custom fusion | bytes 1049088 | tf_op jit(solution)/shard_map/gather | solution.py:110
  457.3 6.1 %gather_fusion.6 = bf16[128,2048]{1,0:T(8,128)(2,1)} fusion(bf16[1536,2048]{1,0:T(8,128)(2,1)} %bitcast.24, s32[1024]{0:T(1024)S(1)} %get-tuple-element.39), kind=kCustom, calls=%fused_computation.6 | custom fusion | bytes 1049088 | tf_op jit(solution)/shard_map/gather | solution.py:110
  463.3 5.8 %gather_fusion.7 = bf16[128,2048]{1,0:T(8,128)(2,1)} fusion(bf16[1536,2048]{1,0:T(8,128)(2,1)} %bitcast.24, s32[1024]{0:T(1024)S(1)} %get-tuple-element.38), kind=kCustom, calls=%fused_computation.7 | custom fusion | bytes 1049088 | tf_op jit(solution)/shard_map/gather | solution.py:110
  469.1 3.9 add_convert_fusion
  (32 shorter events, 0.2 us)
Async XLA Ops:
  6.5 262.4 %copy-start = (bf16[1,512,2048]{2,1,0:T(8,128)(2,1)S(1)}, bf16[1,512,2048]{2,1,0:T(8,128)(2,1)}, u32[]{:S(2)}) copy-start(bf16[1,512,2048]{2,1,0:T(8,128)(2,1)} %param.21) | copy-start | bytes 6291460
  6.5 102.4 %all-gather.2.cloned.1.call-start = ((), (), s32[]{:S(2)}) async-start(), calls=%async_computation.2 | async-start | bytes 8650752 | tf_op jit(solution)/shard_map/all_gather | solution.py:77
  9.2 27.0 %collective-permute-start = (bf16[1]{0:T(256)(128)(2,1)}, bf16[1]{0:T(256)(128)(2,1)}, u32[]{:S(2)}, u32[]{:S(2)}) collective-permute-start(bf16[1]{0:T(256)(128)(2,1)} %bitcast.8), channel_id=1, source_target_pairs={{0,32},{32,0},{64,96},{96,64},{128,160},{160,128},{192,224},{224,1... | collective-permute-start | bytes 14 | tf_op jit(solution)/shard_map/ppermute | solution.py:21
  13.4 23.5 %collective-permute-start.1 = (bf16[2,128,2048]{1,2,0:T(8,128)(2,1)}, bf16[2,128,2048]{1,2,0:T(8,128)(2,1)}, u32[]{:S(2)}, u32[]{:S(2)}) collective-permute-start(bf16[2,128,2048]{1,2,0:T(8,128)(2,1)} %bitcast.127), channel_id=1, source_target_pairs={{0,32},{32,0},{64,96},{96,64},{128,160},{160,128},{192,224},{224,1... | collective-permute-start | bytes 3145736 | tf_op jit(solution)/shard_map/ppermute | solution.py:21
  17.9 7.8 %copy-start.6 = (s32[128,8]{0,1:T(8,128)S(1)}, s32[128,8]{0,1:T(8,128)}, u32[]{:S(2)}) copy-start(s32[128,8]{0,1:T(8,128)} %param.18) | copy-start | bytes 12292
  34.2 1.4 copy-start.1
  34.2 4.2 copy-start.3
  36.2 3.0 copy-start.4
  36.9 2.3 copy-start.2
  36.9 2.3 copy-start.5
  108.9 5.0 %copy-start.7 = (f32[2048]{0:T(1024)S(1)}, f32[2048]{0:T(1024)}, u32[]{:S(2)}) copy-start(f32[2048]{0:T(1024)} %param.17) | copy-start | bytes 24580
  115.8 146.3 %copy-start.9 = (bf16[1,2048,1024]{2,1,0:T(8,128)(2,1)S(1)}, bf16[1,2048,1024]{2,1,0:T(8,128)(2,1)}, u32[]{:S(2)}) copy-start(bf16[1,2048,1024]{2,1,0:T(8,128)(2,1)} %param.20) | copy-start | bytes 12582916
  274.3 7.3 %copy-start.8 = (f32[128,8]{0,1:T(8,128)S(1)}, f32[128,8]{0,1:T(8,128)}, u32[]{:S(2)}) copy-start(f32[128,8]{0,1:T(8,128)} %param.19) | copy-start | bytes 12292
  274.3 147.9 %all-to-all-start.1 = ((bf16[32,48,2048]{2,1,0:T(8,128)(2,1)}), bf16[32,48,2048]{2,1,0:T(8,128)(2,1)}, u32[]{:S(2)}, u32[]{:S(2)}) async-start(bf16[32,48,2048]{2,1,0:T(8,128)(2,1)} %bitcast.121), calls=%async_computation.1 | async-start | bytes 12582912 | tf_op jit(solution)/shard_map/all_to_all | solution.py:106
Sparse Core Ops, SparseCore 0:
  10.0 98.9 all-gather.1
where the time goes:
time: 490 us; the launch traced here: 480 us
  waiting for transfers between devices  209 us (43%)
  blocking collectives  146 us (30%)
  local copies, waits for them, and re-layouts  66.1 us (13%)
  matrix products  23.3 us (5%)
  between operations  15.3 us (3%)
  other arithmetic  11.2 us (2%)
  starting transfers between devices  8.8 us (2%)
    all_to_all x1, blocking collectives, shards(): lax.all_to_all(outgoing, 'expert', split_axis=0, concat_axis=0, tiled=True)  146 us
    all_to_all x1, waiting for transfers between devices, shards(): lax.all_to_all(output_rows, 'expert', split_axis=0, concat_axis=0, tiled=...  141 us
    all_gather x1, waiting for transfers between devices, shards(): lax.all_gather(o_rows, 'expert', axis=0, tiled=True)  67.7 us
    gather x8, local copies, waits for them, and re-layouts, shards(): picked = returned_rows[flat_slot[:, route_k]].astype(jnp.float32)  47 us
  transfers between devices with their start and end apart: 4, of which 2 were waited for; matrix products, arithmetic and copies ran while one was open for 6% of the time, Pallas kernels for 0%

commit v1 on v0

v1 whole, which is shorter than its diff:
```python
import functools
import math

import jax
import jax.numpy as jnp
from jax import lax
from jax.experimental import pallas as pl
from jax.experimental.pallas import tpu as pltpu
from jax.sharding import PartitionSpec as P

HEADS = 16
HD = 128
FF = 512
TOPK = 8
CAP = 48
NX, NY, NZ = 4, 4, 8
EXPERTS = NY * NZ
D = 2048
SPAN = 128
HALF = D // 2
MESH = pl.DeviceIdType.MESH
F32, BF16 = jnp.float32, jnp.bfloat16


def layer_kernel(
    small, gain, resid, queries, span_kv, cache_kv, o_rows, w_in, w_out, out,
    qb, kv, segs, obuf, att, pr, prs, res, tok, mt, wi, wo, xs, hb, rbuf,
    loc, osem_s, osem_r, zsem_s, zsem_r, msem_s, msem_r, isem_s, isem_r, xsem_s, xsem_r,
    usem_s, usem_r, csem_s, csem_r, tsem_s, tsem_r, rsem_s, rsem_r,
):
    g, e = lax.axis_index("group"), lax.axis_index("expert")
    x, c = g // 2, g % 2
    y, z = e // NZ, e % NZ
    f = 1 - 2 * c

    def ring(v, by, n):
        return lax.rem(v + by + 2 * n, n)

    def at(dx=0, dc=0, dy=0, dz=0):
        return (ring(x, dx, NX) * 2 + ring(c, dc, 2), ring(y, dy, NY) * NZ + ring(z, dz, NZ))

    sib = at(dc=1)
    peers = [sib]
    for way in (1, -1):
        peers += [at(dx=way), at(dy=way), at(dz=way)]
    barrier = pltpu.get_barrier_semaphore()
    for peer in peers:
        pl.semaphore_signal(barrier, inc=1, device_id=peer, device_id_type=MESH)

    def remote(src, dst, send, recv, peer):
        return pltpu.make_async_remote_copy(
            src_ref=src, dst_ref=dst, send_sem=send, recv_sem=recv, device_id=peer, device_id_type=MESH
        )

    local = [
        pltpu.make_async_copy(queries, qb, loc.at[0]),
        pltpu.make_async_copy(span_kv, kv.at[:, 0], loc.at[1]),
        pltpu.make_async_copy(cache_kv.at[:, 0, 0], kv.at[:, 1], loc.at[2]),
        pltpu.make_async_copy(o_rows.at[:, pl.ds(c * HALF, HALF)], obuf.at[y, z], loc.at[3]),
        pltpu.make_async_copy(w_in.at[0], wi.at[y], loc.at[4]),
        pltpu.make_async_copy(w_out.at[0], wo.at[y], loc.at[5]),
    ]
    for copy in (local[3], local[0], local[1], local[2]):
        copy.start()
    pl.semaphore_wait(barrier, len(peers))

    started = []

    def go(copy):
        copy.start()
        started.append(copy)
        return copy

    c_kv = go(remote(cache_kv.at[:, 0, 1], kv.at[:, 2], csem_s.at[0], csem_r.at[0], sib))
    c_seg = go(remote(small.at[pl.ds(16, 8)], segs, csem_s.at[1], csem_r.at[1], sib))

    def ring_slots(me, n):
        return [ring(me, -k * f, n) for k in range(n // 2 + 1)], [ring(me, k * f, n) for k in range(n // 2)]

    ys_f, ys_b = ring_slots(y, NY)
    zs_f, zs_b = ring_slots(z, NZ)
    xs_f, xs_b = ring_slots(x, NX)
    y_f, y_b = at(dy=f), at(dy=-f)
    z_f, z_b = at(dz=f), at(dz=-f)
    x_f, x_b = at(dx=f), at(dx=-f)

    class Ring:
        def __init__(self, n, view, own, slots_f, slots_b, to_f, to_b, ss, rs, base=0):
            self.n, self.view, self.slots_f, self.slots_b = n, view, slots_f, slots_b
            self.to_f, self.to_b, self.ss, self.rs, self.base = to_f, to_b, ss, rs, base
            self.own = own
            self.f, self.b = {}, {}

        def put_f(self, k):
            src = self.own if k == 0 else self.view(self.slots_f[k])
            i = self.base + k
            self.f[k + 1] = go(remote(src, self.view(self.slots_f[k]), self.ss.at[i], self.rs.at[i], self.to_f))

        def put_b(self, k):
            src = self.own if k == 0 else self.view(self.slots_b[k])
            i = self.base + self.n // 2 + k
            self.b[k + 1] = go(remote(src, self.view(self.slots_b[k]), self.ss.at[i], self.rs.at[i], self.to_b))

        def start(self):
            self.put_f(0)
            self.put_b(0)

        def step_f(self, k):
            self.f[k].wait_recv()
            if k < self.n // 2:
                self.put_f(k)

        def step_b(self, k):
            self.b[k].wait_recv()
            if k < self.n // 2 - 1:
                self.put_b(k)

    o_y = Ring(NY, lambda s: obuf.at[s, z], o_rows.at[:, pl.ds(c * HALF, HALF)], ys_f, ys_b, y_f, y_b, osem_s, osem_r)
    o_y.start()

    lanes_e = lax.broadcasted_iota(jnp.int32, (EXPERTS, SPAN), 0).astype(F32)
    hit = jnp.zeros((EXPERTS, SPAN), F32)
    wts = jnp.zeros((EXPERTS, SPAN), F32)
    for k in range(TOPK):
        same = lanes_e == small[k : k + 1, :]
        hit = jnp.where(same, 1.0, hit)
        wts = jnp.where(same, small[8 + k : 9 + k, :], wts)
    rows_t = lax.broadcasted_iota(jnp.int32, (SPAN, SPAN), 0)
    cols_t = lax.broadcasted_iota(jnp.int32, (SPAN, SPAN), 1)
    earlier = (rows_t < cols_t).astype(F32).astype(BF16)
    before = jnp.dot(hit.astype(BF16), earlier, preferred_element_type=F32)
    pos = jnp.where(hit > 0.5, before, -1.0)
    for yy in range(NY):
        for zz in range(NZ):
            j = yy * NZ + zz
            mt[z, zz, yy : yy + 1, :] = pos[j : j + 1, :]
            mt[z, zz, 4 + yy : 5 + yy, :] = wts[j : j + 1, :]
    m_z = Ring(NZ, lambda s: mt.at[s], mt.at[z], zs_f, zs_b, z_f, z_b, msem_s, msem_r)
    m_z.start()

    i_y = Ring(NY, lambda s: wi.at[s, x, c], w_in.at[0, x, c], ys_f, ys_b, y_f, y_b, isem_s, isem_r)
    u_y = Ring(NY, lambda s: wo.at[s, c], w_out.at[0, c], ys_f, ys_b, y_f, y_b, usem_s, usem_r)
    others = [ys_f[1], ys_b[1], ys_f[2]]
    i_x = [
        Ring(NX, functools.partial(lambda yy, s: wi.at[yy, s, c], yy), wi.at[yy, x, c], xs_f, xs_b, x_f, x_b, xsem_s, xsem_r, base=3 * i)
        for i, yy in enumerate(others)
    ]
    w_sib = {}

    def share_in(i):
        yy = others[i]
        w_sib[i] = go(remote(wi.at[yy, :, c], wi.at[yy, :, c], csem_s.at[4 + i], csem_r.at[4 + i], sib))

    def share_out(i):
        yy = others[i]
        w_sib[3 + i] = go(remote(wo.at[yy, c], wo.at[yy, c], csem_s.at[7 + i], csem_r.at[7 + i], sib))

    for copy in local[:3]:
        copy.wait()
    o_y.step_f(1)
    o_y.step_b(1)
    i_y.start()
    local[4].start()
    local[5].start()
    c_kv.wait_recv()
    c_seg.wait_recv()

    lane = lax.broadcasted_iota(jnp.int32, (1, SPAN), 1).astype(F32)
    valid = jnp.concatenate(
        [jnp.ones((1, SPAN), F32), (lane < small[16:17, :]).astype(F32), (lane < segs[1:2, :]).astype(F32)], axis=1
    )

    def head(h, carry):
        cols = pl.ds(pl.multiple_of(h * HD, HD), HD)
        q = qb[:, cols]
        keys = kv[0, :, :, cols].reshape(3 * SPAN, HD)
        vals = kv[1, :, :, cols].reshape(3 * SPAN, HD)
        s = lax.dot_general(q, keys, (((1,), (1,)), ((), ())), preferred_element_type=F32) * (1.0 / math.sqrt(HD))
        s = jnp.where(valid > 0.5, s, -1e30)
        m = jnp.max(s, axis=-1, keepdims=True)
        w = jnp.exp(s - m)
        total = jnp.sum(w, axis=-1, keepdims=True)
        a = jnp.dot(w.astype(BF16), vals, preferred_element_type=F32)
        att[c, :, cols] = (a / total).astype(BF16)
        return carry

    def heads(lo, hi):
        lax.fori_loop(lo, hi, head, 0)

    o_z = Ring(NZ, lambda s: obuf.at[:, s], obuf.at[:, z], zs_f, zs_b, z_f, z_b, zsem_s, zsem_r)
    heads(0, 4)
    o_y.step_f(2)
    local[3].wait()
    o_z.start()
    m_z.step_f(1)
    m_z.step_b(1)
    heads(4, 8)
    m_z.step_f(2)
    m_z.step_b(2)
    heads(8, 12)
    m_z.step_f(3)
    m_z.step_b(3)
    heads(12, 16)
    c_att = go(remote(att.at[c], att.at[c], csem_s.at[2], csem_r.at[2], sib))
    i_y.step_f(1)
    i_y.step_b(1)
    i_x[0].start()
    i_x[1].start()
    u_y.start()
    o_z.step_f(1)
    o_z.step_b(1)
    i_y.step_f(2)
    i_x[2].start()
    o_z.step_f(2)
    o_z.step_b(2)
    i_x[0].step_f(1)
    i_x[0].step_b(1)
    u_y.step_f(1)
    u_y.step_b(1)
    share_out(0)
    share_out(1)
    i_x[1].step_f(1)
    i_x[1].step_b(1)
    o_z.step_f(3)
    o_z.step_b(3)
    m_z.step_f(4)
    c_att.wait_recv()
    i_x[2].step_f(1)
    i_x[2].step_b(1)
    o_z.step_f(4)

    both = att[...].reshape(2 * SPAN, D)

    def project(n, carry):
        cols = pl.ds(pl.multiple_of(n * 256, 256), 256)
        got = jnp.dot(both, obuf[:, :, :, cols].reshape(D, 256), preferred_element_type=F32)
        prs[:, :, cols] = got.reshape(2, SPAN, 256)
        return carry

    lax.fori_loop(0, HALF // 256, project, 0)
    c_pr = go(remote(prs.at[1 - c], pr, csem_s.at[3], csem_r.at[3], sib))
    pltpu.sync_copy(resid, qb)
    c_pr.wait_recv()
    mine = prs[c]
    theirs = pr[...]
    first = c == 0
    low = qb[:, :HALF].astype(F32) + jnp.where(first, mine, theirs)
    high = qb[:, HALF:].astype(F32) + jnp.where(first, theirs, mine)
    squares = jnp.sum(low * low, axis=-1, keepdims=True) + jnp.sum(high * high, axis=-1, keepdims=True)
    scale = lax.rsqrt(squares * (1.0 / D) + 1e-05)
    res[:, :HALF] = low
    res[:, HALF:] = high
    tok[z, :, :HALF] = (low * scale * gain[:, :HALF]).astype(BF16)
    tok[z, :, HALF:] = (high * scale * gain[:, HALF:]).astype(BF16)
    t_z = Ring(NZ, lambda s: tok.at[s], tok.at[z], zs_f, zs_b, z_f, z_b, tsem_s, tsem_r)
    t_z.start()

    slot = lax.broadcasted_iota(jnp.int32, (CAP, SPAN), 0).astype(F32)

    def place(src, i):
        pick = jnp.concatenate(
            [jnp.where(slot == mt[src, z, yy : yy + 1, :], 1.0, 0.0) for yy in range(NY)], axis=0
        ).astype(BF16)

        def tile(n, carry):
            cols = pl.ds(pl.multiple_of(n * 512, 512), 512)
            rows = jnp.dot(pick, tok[src, :, cols], preferred_element_type=F32).astype(BF16)
            for yy in range(NY):
                xs[yy, i * CAP : (i + 1) * CAP, cols] = rows[yy * CAP : (yy + 1) * CAP]
            return carry

        lax.fori_loop(0, D // 512, tile, 0)

    def mlp(yy, lo, hi):
        part = slice(lo * CAP, hi * CAP)
        count = (hi - lo) * CAP

        def up(n, carry):
            gate = pl.ds(pl.multiple_of(n * 256, 256), 256)
            lift = pl.ds(pl.multiple_of(FF + n * 256, 256), 256)
            rows = xs[yy, part, :]
            a = jnp.dot(rows, wi[yy, :, :, :, gate].reshape(D, 256), preferred_element_type=F32)
            b = jnp.dot(rows, wi[yy, :, :, :, lift].reshape(D, 256), preferred_element_type=F32)
            hb[:count, gate] = (a * (1.0 / (1.0 + jnp.exp(-a))) * b).astype(BF16)
            return carry

        lax.fori_loop(0, FF // 256, up, 0)

        def down(n, carry):
            cols = pl.ds(pl.multiple_of(n * 512, 512), 512)
            xs[yy, part, cols] = jnp.dot(
                hb[:count, :], wo[yy, :, :, cols].reshape(FF, 512), preferred_element_type=F32
            ).astype(BF16)
            return carry

        lax.fori_loop(0, D // 512, down, 0)

    def combine(src, i, store):
        w = jnp.concatenate(
            [
                jnp.where(slot == mt[src, z, yy : yy + 1, :], mt[src, z, 4 + yy : 5 + yy, :], 0.0)
                for yy in range(NY)
            ],
            axis=0,
        )
        high = w.astype(BF16)
        low = (w - high.astype(F32)).astype(BF16)
        dims = (((0,), (0,)), ((), ()))

        def tile(n, carry):
            cols = pl.ds(pl.multiple_of(n * 512, 512), 512)
            rows = xs[:, i * CAP : (i + 1) * CAP, cols].reshape(NY * CAP, 512)
            got = lax.dot_general(high, rows, dims, preferred_element_type=F32)
            got += lax.dot_general(low, rows, dims, preferred_element_type=F32)
            store(cols, got)
            return carry

        lax.fori_loop(0, D // 512, tile, 0)

    order = [y] + others
    sources = [z, zs_f[1], zs_b[1], zs_f[2], zs_b[2], zs_f[3], zs_b[3], zs_f[4]]

    place(sources[0], 0)
    local[4].wait()
    local[5].wait()
    u_y.step_f(2)
    share_out(2)
    i_x[0].step_f(2)
    share_in(0)
    t_z.step_f(1)
    t_z.step_b(1)
    place(sources[1], 1)
    place(sources[2], 2)
    i_x[1].step_f(2)
    share_in(1)
    t_z.step_f(2)
    t_z.step_b(2)
    i_x[2].step_f(2)
    share_in(2)
    place(sources[3], 3)
    place(sources[4], 4)
    mlp(y, 0, 5)
    for i, came in enumerate((1, 0, 2)):
        w_sib[came].wait_recv()
        w_sib[3 + came].wait_recv()
        mlp(others[i], 0, 5)
    t_z.step_f(3)
    t_z.step_b(3)
    place(sources[5], 5)
    place(sources[6], 6)

    def mlp_all(lo, hi):
        def one(i, carry):
            mlp(ring(y, i, NY), lo, hi)
            return carry

        lax.fori_loop(0, NY, one, 0)

    mlp_all(5, 7)

    for copies in (t_z.f, t_z.b):
        for copy in copies.values():
            copy.wait_send()

    back_f, back_b = {}, {}

    def send_f(k):
        i = k - 1
        back_f[k - 1] = go(remote(tok.at[zs_f[k]], rbuf.at[i], rsem_s.at[i], rsem_r.at[i], z_b))

    def send_b(k):
        i = 4 + k - 1
        back_b[k - 1] = go(remote(tok.at[zs_b[k]], rbuf.at[i], rsem_s.at[i], rsem_r.at[i], z_f))

    def only(dest):
        def store(cols, got):
            tok[dest, :, cols] = got.astype(BF16)

        return store

    def added(dest, slot_at):
        def store(cols, got):
            tok[dest, :, cols] = (got + rbuf[slot_at, :, cols].astype(F32)).astype(BF16)

        return store

    combine(zs_b[3], 6, only(zs_b[3]))
    send_b(3)
    t_z.step_f(4)
    place(sources[7], 7)
    mlp_all(7, 8)
    combine(zs_f[4], 7, only(zs_f[4]))
    send_f(4)

    def hop_b(k, i):
        back_b[k].wait_recv()
        combine(zs_b[k], i, added(zs_b[k], 4 + k))
        send_b(k)

    def hop_f(k, i):
        back_f[k].wait_recv()
        combine(zs_f[k], i, added(zs_f[k], k))
        send_f(k)

    hop_b(2, 4)
    hop_f(3, 5)
    hop_b(1, 2)
    hop_f(2, 3)
    hop_f(1, 1)

    def own(cols, got):
        res[:, cols] = res[:, cols] + got

    combine(z, 0, own)
    back_b[0].wait_recv()
    back_f[0].wait_recv()
    out[...] = (res[...] + rbuf[0].astype(F32) + rbuf[4].astype(F32)).astype(BF16)
    waited = {id(copy) for ring_of in (t_z.f, t_z.b) for copy in ring_of.values()}
    for copy in started:
        if id(copy) not in waited:
            copy.wait_send()


def shards(resid, queries, span_kv, cache_kv, seg_len, o_rows, norm_gain, routes, route_wts, w_in, w_out):
    lens = jnp.broadcast_to(seg_len.astype(F32).T, (2, SPAN))
    small = jnp.concatenate([routes.astype(F32).T, route_wts.T, lens, jnp.zeros((6, SPAN), F32)], axis=0)
    hbm = pl.BlockSpec(memory_space=pl.ANY)
    vmem = pl.BlockSpec(memory_space=pltpu.VMEM)
    dma = pltpu.SemaphoreType.DMA
    return pl.pallas_call(
        layer_kernel,
        out_shape=jax.ShapeDtypeStruct((SPAN, D), BF16),
        in_specs=[vmem, vmem] + [hbm] * 7,
        out_specs=vmem,
        scratch_shapes=[
            pltpu.VMEM((SPAN, D), BF16),
            pltpu.VMEM((2, 3, SPAN, D), BF16),
            pltpu.VMEM((8, SPAN), F32),
            pltpu.VMEM((NY, NZ, D // EXPERTS, HALF), BF16),
            pltpu.VMEM((2, SPAN, D), BF16),
            pltpu.VMEM((SPAN, HALF), F32),
            pltpu.VMEM((2, SPAN, HALF), F32),
            pltpu.VMEM((SPAN, D), F32),
            pltpu.VMEM((NZ, SPAN, D), BF16),
            pltpu.VMEM((NZ, NZ, 8, SPAN), F32),
            pltpu.VMEM((NY, NX, 2, D // 8, 2 * FF), BF16),
            pltpu.VMEM((NY, 2, FF // 2, D), BF16),
            pltpu.VMEM((NY, NZ * CAP, D), BF16),
            pltpu.VMEM((5 * CAP, FF), BF16),
            pltpu.VMEM((7, SPAN, D), BF16),
            dma((6,)),
            dma((3,)), dma((3,)),
            dma((7,)), dma((7,)),
            dma((7,)), dma((7,)),
            dma((3,)), dma((3,)),
            dma((9,)), dma((9,)),
            dma((3,)), dma((3,)),
            dma((10,)), dma((10,)),
            dma((7,)), dma((7,)),
            dma((7,)), dma((7,)),
        ],
        compiler_params=pltpu.CompilerParams(collective_id=0, has_side_effects=True, vmem_limit_bytes=62 << 20),
    )(
        small,
        norm_gain.reshape(1, D),
        resid,
        queries,
        span_kv,
        cache_kv,
        o_rows,
        w_in.reshape(1, NX, 2, D // 8, 2 * FF),
        w_out.reshape(1, 2, FF // 2, D),
    )


def solution(mesh):
    rows = P(("group", "expert"), None)
    placed = (
        rows,
        rows,
        P(None, ("group", "expert"), None),
        P(None, ("group", "expert"), None, None, None),
        rows,
        P("expert", None),
        P(),
        rows,
        rows,
        P("expert", None, None),
        P("expert", None, None),
    )
    return jax.shard_map(shards, mesh=mesh, in_specs=placed, out_specs=rows, check_vma=False)
```

time: 490 us -> 189 us (0.39)
  the two profiles are of different devices: /device:TPU:33 before, /device:TPU:2 now
where the time goes in v1:
time: 189 us; the launch traced here: 188 us
  Pallas kernels  183 us (97%)
  other arithmetic  2.7 us (1%)
  local copies, waits for them, and re-layouts  2.04 us (1%)
    pallas_call x1, Pallas kernels, shards(): pl.pallas_call(layer_kernel, out_shape=jax.ShapeDtypeStruct((SPAN, D), BF...  183 us

profile of v1, /device:TPU:2, one launch (start us, length us, event | category | flops | bytes accessed | tf_op | source)
XLA Modules:
  0.0 188.2 jit_solution(2011275011995801605)
XLA Ops:
  0.0 0.7 convert_bitcast_fusion.1
  0.7 0.1 pad.2.clone
  0.7 0.1 pad.3.clone
  0.8 0.7 convert_bitcast_fusion
  1.5 1.4 maximum_maximum_fusion.small
  2.9 183.5 %shard_map.109 = bf16[128,2048]{1,0:T(8,128)(2,1)} custom-call(f32[24,128]{1,0:T(8,128)} %maximum_maximum_fusion.small, f32[1,2048]{1,0:T(1,128)} %bitcast.10, bf16[128,2048]{1,0:T(8,128)(2,1)} %resid.1, bf16[128,2048]{1,0:T(8,128)(2,1)} %queries.1, bf16[2,128,2048]{2,1,0:T(8,128)(2,1)} %span_kv.1, bf16[2,1,2,128,2048]{4,3,2,1,0:T(8,128)(2,1)} %cache_kv.1, ...), custom_call_target="tpu_custom_call" | custom-call | tf_op jit(solution)/shard_map/pallas_call | solution.py:430
  186.3 1.9 copy.13
  (1 shorter events, 0.0 us)

commit v2 on v1

v2 whole, which is shorter than its diff:
```python
import functools
import math

import jax
import jax.numpy as jnp
from jax import lax
from jax.experimental import pallas as pl
from jax.experimental.pallas import tpu as pltpu
from jax.sharding import PartitionSpec as P

HEADS = 16
HD = 128
FF = 512
TOPK = 8
CAP = 48
NX, NY, NZ = 4, 4, 8
EXPERTS = NY * NZ
D = 2048
SPAN = 128
HALF = D // 2
OX = 128
OZ = HALF - NX * OX
WY = 512
PIECE = 512
MESH = pl.DeviceIdType.MESH
F32, BF16 = jnp.float32, jnp.bfloat16


def layer_kernel(
    routes, route_wts, seg_len, gain, resid, queries, span_kv, cache_kv, o_rows, w_in, w_out, out,
    qb, kv, segs, seg_out, obuf, att, pr, prs, res, tok, mine_t, mt, wiy, wix, wo, xs, hb, rbuf, loc, sent, came,
):
    g, e = lax.axis_index("group"), lax.axis_index("expert")
    x, c = g // 2, g % 2
    y, z = e // NZ, e % NZ
    f = 1 - 2 * c

    def ring(v, by, n):
        return lax.rem(v + by + 2 * n, n)

    def at(dx=0, dc=0, dy=0, dz=0):
        return (ring(x, dx, NX) * 2 + ring(c, dc, 2), ring(y, dy, NY) * NZ + ring(z, dz, NZ))

    sib = at(dc=1)
    x_peers = [at(dx=k) for k in (1, NX - 1, 2)]
    y_peers = [at(dy=k) for k in (1, NY - 1, 2)]
    z_peers = [at(dz=k) for k in range(1, NZ)]
    peers = [sib] + x_peers + y_peers + z_peers
    barrier = pltpu.get_barrier_semaphore()
    for peer in peers:
        pl.semaphore_signal(barrier, inc=1, device_id=peer, device_id_type=MESH)

    half = c * HALF
    local = [
        pltpu.make_async_copy(o_rows.at[:, pl.ds(half, OZ)], obuf.at[0, z, :, pl.ds(0, OZ)], loc.at[0]),
        pltpu.make_async_copy(o_rows.at[:, pl.ds(half + OZ + x * OX, OX)], obuf.at[0, z, :, pl.ds(OZ, OX)], loc.at[1]),
        pltpu.make_async_copy(queries, qb, loc.at[2]),
        pltpu.make_async_copy(span_kv, kv.at[:, 0], loc.at[3]),
        pltpu.make_async_copy(cache_kv.at[:, 0, 0], kv.at[:, 1], loc.at[4]),
        pltpu.make_async_copy(w_in.at[:, pl.ds(0, WY)], wiy.at[pl.ds(y, 1)], loc.at[5]),
        pltpu.make_async_copy(w_in.at[:, pl.ds(WY, D - WY)], wix.at[pl.ds(y, 1)], loc.at[6]),
        pltpu.make_async_copy(w_out, wo.at[pl.ds(y, 1)], loc.at[7]),
    ]
    for copy in local[:5]:
        copy.start()
    seg_out[...] = jnp.broadcast_to(seg_len[:, 1:2].astype(F32), seg_out.shape)
    pl.semaphore_wait(barrier, len(peers))

    started, used, done = [], [0], set()

    def remote(src, dst, peer, slot=None):
        i = used[0] if slot is None else slot
        used[0] += slot is None
        copy = pltpu.make_async_remote_copy(
            src_ref=src, dst_ref=dst, send_sem=sent.at[i], recv_sem=came.at[i], device_id=peer, device_id_type=MESH
        )
        copy.start()
        started.append(copy)
        return copy

    def gone(copy):
        copy.wait_send()
        done.add(id(copy))

    def slots(n):
        i = used[0]
        used[0] += n
        return i

    def ring_slots(me, n):
        return [ring(me, -k * f, n) for k in range(n // 2 + 1)], [ring(me, k * f, n) for k in range(n // 2)]

    ys_f, ys_b = ring_slots(y, NY)
    zs_f, zs_b = ring_slots(z, NZ)
    xs_f, xs_b = ring_slots(x, NX)
    to_y, to_z, to_x = (at(dy=f), at(dy=-f)), (at(dz=f), at(dz=-f)), (at(dx=f), at(dx=-f))

    class Ring:
        def __init__(self, n, view, slots_f, slots_b, to, own=None, view_to=None):
            self.n, self.view, self.slots_f, self.slots_b, self.to = n, view, slots_f, slots_b, to
            self.own = view(slots_f[0]) if own is None else own
            self.view_to = view_to or (lambda s, way: view(s))
            self.base = slots(n - 1)
            self.f, self.b = {}, {}

        def put_f(self, k):
            src = self.own if k == 0 else self.view(self.slots_f[k])
            self.f[k + 1] = remote(src, self.view_to(self.slots_f[k], f), self.to[0], self.base + k)

        def put_b(self, k):
            src = self.own if k == 0 else self.view(self.slots_b[k])
            self.b[k + 1] = remote(src, self.view_to(self.slots_b[k], -f), self.to[1], self.base + self.n // 2 + k)

        def start(self):
            self.put_f(0)
            self.put_b(0)

        def step_f(self, k):
            self.f[k].wait_recv()
            if k < self.n // 2:
                self.put_f(k)

        def step_b(self, k):
            self.b[k].wait_recv()
            if k < self.n // 2 - 1:
                self.put_b(k)

        def step(self, k):
            self.step_f(k)
            if k < self.n // 2:
                self.step_b(k)

    zx = pl.ds(0, OZ + OX)
    local[0].wait()
    local[1].wait()
    o_y = [
        remote(obuf.at[0, z, :, zx], obuf.at[NY - k, z, :, zx], peer) for k, peer in zip((1, NY - 1, 2), y_peers)
    ]
    c_kv = remote(cache_kv.at[:, 0, 1], kv.at[:, 2], sib)
    c_seg = remote(seg_out, segs, sib)

    chunks = [pl.ds(OZ, OX)] + [pl.ds(k * (OZ // 2), OZ // 2) for k in range(2)]
    o_z = [Ring(NZ, functools.partial(lambda cols, s: obuf.at[:, s, :, cols], cols), zs_f, zs_b, to_z) for cols in chunks]
    o_x = []

    def spread(zz):
        for k, peer in zip((1, NX - 1, 2), x_peers):
            there = pl.ds(OZ + (NX - k) * OX, OX)
            o_x.append(remote(obuf.at[:, zz, :, chunks[0]], obuf.at[:, zz, :, there], peer))

    others = [ys_f[1], ys_b[1], ys_f[2]]
    deep = (D - WY) // 8

    def shard(s, start=0):
        return pl.ds(pl.multiple_of(start + (c * NX + s) * deep, 16), deep)

    def core_half(n):
        return pl.ds(pl.multiple_of(c * (n // 2), 16), n // 2)

    i_y = Ring(NY, lambda s: wix.at[s, shard(x)], ys_f, ys_b, to_y, own=w_in.at[0, shard(x, WY)])
    v_y = Ring(NY, lambda s: wiy.at[s, core_half(WY)], ys_f, ys_b, to_y, own=w_in.at[0, core_half(WY)])
    u_y = Ring(NY, lambda s: wo.at[s, core_half(FF)], ys_f, ys_b, to_y, own=w_out.at[0, core_half(FF)])
    i_x = [
        Ring(NX, functools.partial(lambda yy, s: wix.at[yy, shard(s)], yy), xs_f, xs_b, to_x)
        for yy in others
    ]
    w_sib, w_at = {}, slots(9)

    def share(i, what):
        yy = others[i]
        part = {"x": wix.at[yy, core_half(D - WY)], "y": wiy.at[yy, core_half(WY)], "o": wo.at[yy, core_half(FF)]}[what]
        w_sib[i, what] = remote(part, part, sib, w_at + 3 * i + "xyo".index(what))

    def have(i):
        for what in "yox":
            w_sib[(1, 0, 2)[i], what].wait_recv()

    lanes_e = lax.broadcasted_iota(jnp.int32, (EXPERTS, SPAN), 0).astype(F32)
    hit = jnp.zeros((EXPERTS, SPAN), F32)
    wts = jnp.zeros((EXPERTS, SPAN), F32)
    for k in range(TOPK):
        same = lanes_e == routes[k : k + 1, :].astype(F32)
        hit = jnp.where(same, 1.0, hit)
        wts = jnp.where(same, route_wts[k : k + 1, :], wts)
    rows_t = lax.broadcasted_iota(jnp.int32, (SPAN, SPAN), 0)
    cols_t = lax.broadcasted_iota(jnp.int32, (SPAN, SPAN), 1)
    earlier = (rows_t < cols_t).astype(F32).astype(BF16)
    before = jnp.dot(hit.astype(BF16), earlier, preferred_element_type=F32)
    pos = jnp.where(hit > 0.5, before, -1.0)
    for yy in range(NY):
        for zz in range(NZ):
            j = yy * NZ + zz
            mine_t[zz, yy : yy + 1, :] = pos[j : j + 1, :]
            mine_t[zz, 4 + yy : 5 + yy, :] = wts[j : j + 1, :]
    mt[z] = mine_t[z]
    metas = []
    for k in range(1, NZ):
        metas.append(remote(mine_t.at[ring(z, k, NZ)], mt.at[z], z_peers[k - 1]))

    for copy in local[2:5]:
        copy.wait()
    c_kv.wait_recv()
    c_seg.wait_recv()

    lane = lax.broadcasted_iota(jnp.int32, (1, SPAN), 1).astype(F32)
    valid = jnp.concatenate(
        [jnp.ones((1, SPAN), F32), (lane < seg_len[:, 0:1].astype(F32)).astype(F32), (lane < segs[0:1, :]).astype(F32)], axis=1
    )

    def head(h, carry):
        cols = pl.ds(pl.multiple_of(h * HD, HD), HD)
        q = qb[:, cols]
        keys = kv[0, :, :, cols].reshape(3 * SPAN, HD)
        vals = kv[1, :, :, cols].reshape(3 * SPAN, HD)
        s = lax.dot_general(q, keys, (((1,), (1,)), ((), ())), preferred_element_type=F32) * (1.0 / math.sqrt(HD))
        s = jnp.where(valid > 0.5, s, -1e30)
        m = jnp.max(s, axis=-1, keepdims=True)
        w = jnp.exp(s - m)
        total = jnp.sum(w, axis=-1, keepdims=True)
        a = jnp.dot(w.astype(BF16), vals, preferred_element_type=F32)
        att[c, :, cols] = (a / total).astype(BF16)
        return carry

    def heads(lo, hi):
        lax.fori_loop(lo, hi, head, 0)

    heads(0, 4)
    for copy in o_y:
        copy.wait_recv()
    for o in o_z:
        o.start()
    spread(z)
    i_y.start()
    for copy in local[5:]:
        copy.start()
    heads(4, 12)
    o_z[0].step(1)
    spread(zs_f[1])
    spread(zs_b[1])
    heads(12, 16)
    c_att = remote(att.at[c], att.at[c], sib)
    load = pltpu.make_async_copy(resid, qb, loc.at[2])
    load.start()
    o_z[1].step(1)
    o_z[2].step(1)
    o_z[0].step(2)
    spread(zs_f[2])
    spread(zs_b[2])
    i_y.step(1)
    v_y.start()
    u_y.start()
    o_z[1].step(2)
    o_z[2].step(2)
    o_z[0].step(3)
    spread(zs_f[3])
    spread(zs_b[3])
    i_y.step_f(2)
    o_z[1].step(3)
    o_z[2].step(3)
    o_z[0].step_f(4)
    spread(zs_f[4])
    i_x[0].start()
    i_x[1].start()
    for copy in metas:
        copy.wait_recv()
    c_att.wait_recv()
    o_z[1].step_f(4)
    o_z[2].step_f(4)
    for copy in o_x:
        copy.wait_recv()

    def columns(n):
        cols = pl.ds(pl.multiple_of(n * 256, 256), 256)
        total = jnp.zeros((2 * SPAN, 256), F32)
        for r in range(NY):
            depth = pl.ds(pl.multiple_of(ring(y, r, NY) * (D // NY), D // NY), D // NY)
            rows = att[:, :, depth].reshape(2 * SPAN, D // NY)
            total += jnp.dot(rows, obuf[r, :, :, cols].reshape(D // NY, 256), preferred_element_type=F32)
        return total.reshape(2, SPAN, 256)

    def project_z(n, carry):
        prs[:, :, pl.ds(pl.multiple_of(n * 256, 256), 256)] = columns(n)
        return carry

    def project_x(n):
        got = columns(OZ // 256 + n)
        for i in range(2):
            spot = pl.ds(pl.multiple_of(OZ + ring(x, 2 * n + i, NX) * OX, OX), OX)
            prs[:, :, spot] = got[:, :, i * OX : (i + 1) * OX]

    lax.fori_loop(0, OZ // 256, project_z, 0)
    for n in range(NX * OX // 256):
        project_x(n)
    c_pr = remote(prs.at[1 - c], pr, sib)
    load.wait()
    c_pr.wait_recv()
    mine = prs[c]
    theirs = pr[...]
    first = c == 0
    low = qb[:, :HALF].astype(F32) + jnp.where(first, mine, theirs)
    high = qb[:, HALF:].astype(F32) + jnp.where(first, theirs, mine)
    squares = jnp.sum(low * low, axis=-1, keepdims=True) + jnp.sum(high * high, axis=-1, keepdims=True)
    scale = lax.rsqrt(squares * (1.0 / D) + 1e-05)
    tok[z, :, :HALF] = (low * scale * gain[:, :HALF]).astype(BF16)
    t_z = [Ring(NZ, functools.partial(lambda j, s: tok.at[s, :, pl.ds(j * HALF, HALF)], j), zs_f, zs_b, to_z) for j in range(2)]
    t_z[0].start()
    tok[z, :, HALF:] = (high * scale * gain[:, HALF:]).astype(BF16)
    t_z[1].start()
    res[:, :HALF] = low
    res[:, HALF:] = high

    slot = lax.broadcasted_iota(jnp.int32, (CAP, SPAN), 0).astype(F32)

    def place(src, i):
        pick = jnp.concatenate(
            [jnp.where(slot == mt[src, yy : yy + 1, :], 1.0, 0.0) for yy in range(NY)], axis=0
        ).astype(BF16)

        def tile(n, carry):
            cols = pl.ds(pl.multiple_of(n * 512, 512), 512)
            rows = jnp.dot(pick, tok[src, :, cols], preferred_element_type=F32).astype(BF16)
            for yy in range(NY):
                xs[yy, i * CAP : (i + 1) * CAP, cols] = rows[yy * CAP : (yy + 1) * CAP]
            return carry

        lax.fori_loop(0, D // 512, tile, 0)

    def mlp(yy, lo, hi):
        part = slice(lo * CAP, hi * CAP)
        count = (hi - lo) * CAP

        def up(n, carry):
            gate = pl.ds(pl.multiple_of(n * 256, 256), 256)
            lift = pl.ds(pl.multiple_of(FF + n * 256, 256), 256)

            def times(cols):
                got = jnp.dot(xs[yy, part, :WY], wiy[yy, :, cols], preferred_element_type=F32)
                return got + jnp.dot(xs[yy, part, WY:], wix[yy, :, cols], preferred_element_type=F32)

            a, b = times(gate), times(lift)
            hb[:count, gate] = (a * (1.0 / (1.0 + jnp.exp(-a))) * b).astype(BF16)
            return carry

        lax.fori_loop(0, FF // 256, up, 0)

        def down(n, carry):
            cols = pl.ds(pl.multiple_of(n * 512, 512), 512)
            xs[yy, part, cols] = jnp.dot(
                hb[:count, :], wo[yy, :, cols], preferred_element_type=F32
            ).astype(BF16)
            return carry

        lax.fori_loop(0, D // 512, down, 0)

    def mlps(which, lo, hi):
        lax.fori_loop(which[0], which[1], lambda i, carry: (mlp(ring(y, i, NY), lo, hi), carry)[1], 0)

    dims = (((0,), (0,)), ((), ()))

    def weights(src):
        w = jnp.concatenate(
            [
                jnp.where(slot == mt[src, yy : yy + 1, :], mt[src, 4 + yy : 5 + yy, :], 0.0)
                for yy in range(NY)
            ],
            axis=0,
        )
        top = w.astype(BF16)
        return top, (w - top.astype(F32)).astype(BF16)

    def combined(pair, i, cols):
        rows = xs[:, i * CAP : (i + 1) * CAP, cols].reshape(NY * CAP, PIECE)
        got = lax.dot_general(pair[0], rows, dims, preferred_element_type=F32)
        return got + lax.dot_general(pair[1], rows, dims, preferred_element_type=F32)

    back = {}
    pieces = [pl.ds(j * PIECE, PIECE) for j in range(D // PIECE)]

    def send(way, k, j):
        i = k - 1 + (0 if way == "f" else 4)
        src = (zs_f if way == "f" else zs_b)[k]
        back[way, k - 1, j] = remote(
            tok.at[src, :, pieces[j]], rbuf.at[i, :, pieces[j]], to_z[1] if way == "f" else to_z[0]
        )

    def hop(way, k, i, js=range(D // PIECE)):
        src = (zs_f if way == "f" else zs_b)[k]
        last = k == (4 if way == "f" else 3)
        pair = weights(src)
        for j in js:
            if not last:
                if j == 0:
                    for t in t_z:
                        gone((t.f if way == "f" else t.b)[k + 1])
                back[way, k, j].wait_recv()
            got = combined(pair, i, pieces[j])
            if not last:
                got += rbuf[k + (0 if way == "f" else 4), :, pieces[j]].astype(F32)
            tok[src, :, pieces[j]] = got.astype(BF16)
            send(way, k, j)

    place(z, 0)
    i_x[0].step(1)
    t_z[0].step(1)
    i_x[1].step(1)
    i_x[2].start()
    local[5].wait()
    local[6].wait()
    local[7].wait()
    v_y.step(1)
    share(0, "y")
    share(1, "y")
    t_z[1].step(1)
    place(zs_f[1], 1)
    place(zs_b[1], 2)
    u_y.step(1)
    share(0, "o")
    share(1, "o")
    t_z[0].step(2)
    i_x[0].step_f(2)
    share(0, "x")
    i_x[1].step_f(2)
    share(1, "x")
    t_z[1].step(2)
    place(zs_f[2], 3)
    place(zs_b[2], 4)
    v_y.step_f(2)
    share(2, "y")
    i_x[2].step(1)
    mlp(y, 0, 5)
    t_z[0].step(3)
    have(0)
    mlp(others[0], 0, 5)
    u_y.step_f(2)
    share(2, "o")
    have(1)
    mlp(others[1], 0, 5)
    t_z[1].step(3)
    place(zs_f[3], 5)
    place(zs_b[3], 6)
    i_x[2].step_f(2)
    share(2, "x")
    mlps((NY - 1, NY + 2), 5, 7)
    have(2)
    mlp(others[2], 0, 7)
    hop("b", 3, 6)
    t_z[0].step_f(4)
    t_z[1].step_f(4)
    place(zs_f[4], 7)
    mlps((0, 2), 7, 8)
    hop("b", 2, 4, range(0, 2))
    mlps((2, 3), 7, 8)
    hop("b", 2, 4, range(2, 3))
    mlps((3, 4), 7, 8)
    hop("b", 2, 4, range(3, 4))
    hop("f", 4, 7)
    hop("b", 1, 2, range(0, 2))
    hop("f", 3, 5, range(0, 2))
    hop("b", 1, 2, range(2, 4))
    hop("f", 3, 5, range(2, 4))
    hop("f", 2, 3)
    hop("f", 1, 1)

    pair = weights(z)
    for j in range(D // PIECE):
        res[:, pieces[j]] = res[:, pieces[j]] + combined(pair, 0, pieces[j])
    for j in range(D // PIECE):
        back["b", 0, j].wait_recv()
        back["f", 0, j].wait_recv()
        both = rbuf[0, :, pieces[j]].astype(F32) + rbuf[4, :, pieces[j]].astype(F32)
        out[:, pieces[j]] = (res[:, pieces[j]] + both).astype(BF16)
    for copy in started:
        if id(copy) not in done:
            copy.wait_send()


def shards(resid, queries, span_kv, cache_kv, seg_len, o_rows, norm_gain, routes, route_wts, w_in, w_out):
    hbm = pl.BlockSpec(memory_space=pl.ANY)
    vmem = pl.BlockSpec(memory_space=pltpu.VMEM)
    dma = pltpu.SemaphoreType.DMA
    return pl.pallas_call(
        layer_kernel,
        out_shape=jax.ShapeDtypeStruct((SPAN, D), BF16),
        in_specs=[vmem] * 4 + [hbm] * 7,
        out_specs=vmem,
        scratch_shapes=[
            pltpu.VMEM((SPAN, D), BF16),
            pltpu.VMEM((2, 3, SPAN, D), BF16),
            pltpu.VMEM((8, SPAN), F32),
            pltpu.VMEM((8, SPAN), F32),
            pltpu.VMEM((NY, NZ, D // EXPERTS, HALF), BF16),
            pltpu.VMEM((2, SPAN, D), BF16),
            pltpu.VMEM((SPAN, HALF), F32),
            pltpu.VMEM((2, SPAN, HALF), F32),
            pltpu.VMEM((SPAN, D), F32),
            pltpu.VMEM((NZ, SPAN, D), BF16),
            pltpu.VMEM((NZ, 8, SPAN), F32),
            pltpu.VMEM((NZ, 8, SPAN), F32),
            pltpu.VMEM((NY, WY, 2 * FF), BF16),
            pltpu.VMEM((NY, D - WY, 2 * FF), BF16),
            pltpu.VMEM((NY, FF, D), BF16),
            pltpu.VMEM((NY, NZ * CAP, D), BF16),
            pltpu.VMEM((7 * CAP, FF), BF16),
            pltpu.VMEM((7, SPAN, D), BF16),
            dma((8,)),
            dma((160,)),
            dma((160,)),
        ],
        compiler_params=pltpu.CompilerParams(collective_id=0, has_side_effects=True, vmem_limit_bytes=62 << 20),
    )(
        routes.T,
        route_wts.T,
        seg_len,
        norm_gain.reshape(1, D),
        resid,
        queries,
        span_kv,
        cache_kv,
        o_rows,
        w_in,
        w_out,
    )


def solution(mesh):
    rows = P(("group", "expert"), None)
    placed = (
        rows,
        rows,
        P(None, ("group", "expert"), None),
        P(None, ("group", "expert"), None, None, None),
        rows,
        P("expert", None),
        P(),
        rows,
        rows,
        P("expert", None, None),
        P("expert", None, None),
    )
    return jax.shard_map(shards, mesh=mesh, in_specs=placed, out_specs=rows, check_vma=False)
```

time: 189 us -> 146 us (0.77)
  the two profiles are of different devices: /device:TPU:2 before, /device:TPU:33 now
where the time goes in v2:
time: 146 us; the launch traced here: 144 us
  Pallas kernels  142 us (97%)
  local copies, waits for them, and re-layouts  1.88 us (1%)
    pallas_call x1, Pallas kernels, shards(): pl.pallas_call(layer_kernel, out_shape=jax.ShapeDtypeStruct((SPAN, D), BF...  142 us

profile of v2, /device:TPU:33, one launch (start us, length us, event | category | flops | bytes accessed | tf_op | source)
XLA Modules:
  0.0 143.6 jit_solution(14791303964935533856)
XLA Ops:
  0.0 141.7 %shard_map.109 = bf16[128,2048]{1,0:T(8,128)(2,1)} custom-call(s32[8,128]{1,0:T(8,128)} %bitcast.4, f32[8,128]{1,0:T(8,128)} %bitcast.5, s32[1,2]{1,0:T(1,128)} %seg_len.1, f32[1,2048]{1,0:T(1,128)} %bitcast.3, bf16[128,2048]{1,0:T(8,128)(2,1)} %resid.1, bf16[128,2048]{1,0:T(8,128)(2,1)} %queries.1, bf16[2,128,2048]{2,1,0:T(8,128)(2,1)} %span_kv.1, ...), custom_call_target="tpu_custom_call" | custom-call | tf_op jit(solution)/shard_map/pallas_call | solution.py:481
  141.7 1.9 %copy.13 = bf16[128,2048]{1,0:T(8,128)(2,1)} copy(bf16[128,2048]{1,0:T(8,128)(2,1)} %shard_map.109) | data formatting | bytes 1048576

commit v3 on v2

--- a/solution.py
+++ b/solution.py
@@ -20,7 +20,7 @@
 HALF = D // 2
 OX = 128
 OZ = HALF - NX * OX
-WY = 512
+WY = 640
 PIECE = 512
 MESH = pl.DeviceIdType.MESH
 F32, BF16 = jnp.float32, jnp.bfloat16
@@ -42,7 +42,7 @@
         return (ring(x, dx, NX) * 2 + ring(c, dc, 2), ring(y, dy, NY) * NZ + ring(z, dz, NZ))
 
     sib = at(dc=1)
-    x_peers = [at(dx=k) for k in (1, NX - 1, 2)]
+    x_peers = [at(dx=k) for k in (1, NX - 1)]
     y_peers = [at(dy=k) for k in (1, NY - 1, 2)]
     z_peers = [at(dz=k) for k in range(1, NZ)]
     peers = [sib] + x_peers + y_peers + z_peers
@@ -140,15 +140,35 @@
     c_seg = remote(seg_out, segs, sib)
 
     chunks = [pl.ds(OZ, OX)] + [pl.ds(k * (OZ // 2), OZ // 2) for k in range(2)]
-    o_z = [Ring(NZ, functools.partial(lambda cols, s: obuf.at[:, s, :, cols], cols), zs_f, zs_b, to_z) for cols in chunks]
-    o_x = []
-
-    def spread(zz):
-        for k, peer in zip((1, NX - 1, 2), x_peers):
-            there = pl.ds(OZ + (NX - k) * OX, OX)
-            o_x.append(remote(obuf.at[:, zz, :, chunks[0]], obuf.at[:, zz, :, there], peer))
-
-    others = [ys_f[1], ys_b[1], ys_f[2]]
+    o_own = Ring(NZ, lambda s: obuf.at[0, s, :, zx], zs_f, zs_b, to_z)
+    o_own.start()
+    o_z = [
+        Ring(NZ, functools.partial(lambda cols, s: obuf.at[pl.ds(1, NY - 1), s, :, cols], cols), zs_f, zs_b, to_z)
+        for cols in chunks
+    ]
+    def shard_from(k, way):
+        slots = [(-k * way_f) % NX if way == 0 else (-k * way_f - way * way_f) % NX for way_f in (1, -1)]
+        return pl.ds(pl.multiple_of(OZ + (slots[0] + c * (slots[1] - slots[0])) * OX, OX), OX)
+
+    class Spread:
+        def __init__(self, zz):
+            self.zz = zz
+            self.f1 = self.send(0, 1)
+            self.b1 = self.send(0, -1)
+
+        def send(self, k, way):
+            src, dst = obuf.at[:, self.zz, :, shard_from(k, 0)], obuf.at[:, self.zz, :, shard_from(k, way)]
+            return remote(src, dst, to_x[0] if way == 1 else to_x[1])
+
+        def step(self):
+            self.f1.wait_recv()
+            self.f2 = self.send(1, 1)
+
+        def end(self):
+            self.b1.wait_recv()
+            self.f2.wait_recv()
+
+    others = [ring(y, -1, NY), ring(y, 1, NY), ring(y, 2, NY)]
     deep = (D - WY) // 8
 
     def shard(s, start=0):
@@ -173,7 +193,7 @@
 
     def have(i):
         for what in "yox":
-            w_sib[(1, 0, 2)[i], what].wait_recv()
+            w_sib[i, what].wait_recv()
 
     lanes_e = lax.broadcasted_iota(jnp.int32, (EXPERTS, SPAN), 0).astype(F32)
     hit = jnp.zeros((EXPERTS, SPAN), F32)
@@ -224,50 +244,61 @@
     def heads(lo, hi):
         lax.fori_loop(lo, hi, head, 0)
 
+    i_y.start()
+    v_y.start()
     heads(0, 4)
+    o_own.step(1)
     for copy in o_y:
         copy.wait_recv()
-    for o in o_z:
-        o.start()
-    spread(z)
-    i_y.start()
+    o_z[0].start()
+    s_own = Spread(z)
     for copy in local[5:]:
         copy.start()
-    heads(4, 12)
+    o_own.step(2)
+    heads(4, 7)
     o_z[0].step(1)
-    spread(zs_f[1])
-    spread(zs_b[1])
+    o_z[1].start()
+    s_f1, s_b1 = Spread(zs_f[1]), Spread(zs_b[1])
+    o_z[2].start()
+    heads(7, 9)
+    o_own.step(3)
+    o_z[0].step(2)
+    s_f2, s_b2 = Spread(zs_f[2]), Spread(zs_b[2])
+    s_own.step()
+    o_z[1].step(1)
+    heads(9, 12)
+    o_z[2].step(1)
+    i_y.step(1)
+    u_y.start()
+    o_own.step(4)
+    o_z[0].step(3)
+    s_f3, s_b3 = Spread(zs_f[3]), Spread(zs_b[3])
+    s_f1.step()
+    s_b1.step()
     heads(12, 16)
     c_att = remote(att.at[c], att.at[c], sib)
     load = pltpu.make_async_copy(resid, qb, loc.at[2])
     load.start()
-    o_z[1].step(1)
-    o_z[2].step(1)
-    o_z[0].step(2)
-    spread(zs_f[2])
-    spread(zs_b[2])
-    i_y.step(1)
-    v_y.start()
-    u_y.start()
     o_z[1].step(2)
+    o_z[0].step_f(4)
+    s_f4 = Spread(zs_f[4])
     o_z[2].step(2)
-    o_z[0].step(3)
-    spread(zs_f[3])
-    spread(zs_b[3])
-    i_y.step_f(2)
+    s_f2.step()
+    s_b2.step()
     o_z[1].step(3)
+    s_f3.step()
+    s_b3.step()
+    s_f4.step()
     o_z[2].step(3)
-    o_z[0].step_f(4)
-    spread(zs_f[4])
     i_x[0].start()
-    i_x[1].start()
     for copy in metas:
         copy.wait_recv()
     c_att.wait_recv()
     o_z[1].step_f(4)
     o_z[2].step_f(4)
-    for copy in o_x:
-        copy.wait_recv()
+    for spread in (s_own, s_f1, s_b1, s_f2, s_b2, s_f3, s_b3, s_f4):
+        spread.end()
+    i_x[1].start()
 
     def columns(n):
         cols = pl.ds(pl.multiple_of(n * 256, 256), 256)
@@ -402,6 +433,7 @@
     place(z, 0)
     i_x[0].step(1)
     t_z[0].step(1)
+    i_y.step_f(2)
     i_x[1].step(1)
     i_x[2].start()
     local[5].wait()
@@ -413,51 +445,53 @@
     t_z[1].step(1)
     place(zs_f[1], 1)
     place(zs_b[1], 2)
+    mlp(y, 0, 3)
+    t_z[0].step(2)
+    i_x[0].step_f(2)
+    share(0, "x")
     u_y.step(1)
     share(0, "o")
     share(1, "o")
-    t_z[0].step(2)
-    i_x[0].step_f(2)
-    share(0, "x")
+    t_z[1].step(2)
     i_x[1].step_f(2)
     share(1, "x")
-    t_z[1].step(2)
+    i_x[2].step(1)
     place(zs_f[2], 3)
     place(zs_b[2], 4)
     v_y.step_f(2)
     share(2, "y")
-    i_x[2].step(1)
-    mlp(y, 0, 5)
-    t_z[0].step(3)
     have(0)
     mlp(others[0], 0, 5)
+    t_z[0].step(3)
+    have(1)
+    mlp(others[1], 0, 5)
+    i_x[2].step_f(2)
+    share(2, "x")
+    t_z[1].step(3)
+    place(zs_b[3], 5)
+    mlp(y, 3, 6)
     u_y.step_f(2)
     share(2, "o")
-    have(1)
-    mlp(others[1], 0, 5)
-    t_z[1].step(3)
-    place(zs_f[3], 5)
-    place(zs_b[3], 6)
-    i_x[2].step_f(2)
-    share(2, "x")
-    mlps((NY - 1, NY + 2), 5, 7)
+    mlp(others[0], 5, 6)
+    mlp(others[1], 5, 6)
     have(2)
-    mlp(others[2], 0, 7)
-    hop("b", 3, 6)
+    mlp(others[2], 0, 6)
+    hop("b", 3, 5)
+    place(zs_f[3], 6)
     t_z[0].step_f(4)
     t_z[1].step_f(4)
     place(zs_f[4], 7)
-    mlps((0, 2), 7, 8)
+    mlps((0, 2), 6, 8)
     hop("b", 2, 4, range(0, 2))
-    mlps((2, 3), 7, 8)
+    mlps((2, 3), 6, 8)
     hop("b", 2, 4, range(2, 3))
-    mlps((3, 4), 7, 8)
+    mlps((3, 4), 6, 8)
     hop("b", 2, 4, range(3, 4))
     hop("f", 4, 7)
     hop("b", 1, 2, range(0, 2))
-    hop("f", 3, 5, range(0, 2))
+    hop("f", 3, 6, range(0, 2))
     hop("b", 1, 2, range(2, 4))
-    hop("f", 3, 5, range(2, 4))
+    hop("f", 3, 6, range(2, 4))
     hop("f", 2, 3)
     hop("f", 1, 1)
 
@@ -500,7 +534,7 @@
             pltpu.VMEM((NY, D - WY, 2 * FF), BF16),
             pltpu.VMEM((NY, FF, D), BF16),
             pltpu.VMEM((NY, NZ * CAP, D), BF16),
-            pltpu.VMEM((7 * CAP, FF), BF16),
+            pltpu.VMEM((6 * CAP, FF), BF16),
             pltpu.VMEM((7, SPAN, D), BF16),
             dma((8,)),
             dma((160,)),

time: 146 us -> 143 us (0.979)
  Pallas kernels: 142 us -> 140 us
    pallas_call x1, Pallas kernels: 142 us -> 140 us  [shards(): pl.pallas_call(layer_kernel, out_shape=jax.ShapeDtypeStruct((SPAN, D), BF...]
where the time goes in v3:
time: 143 us; the launch traced here: 142 us
  Pallas kernels  140 us (98%)
  local copies, waits for them, and re-layouts  1.88 us (1%)
    pallas_call x1, Pallas kernels, shards(): pl.pallas_call(layer_kernel, out_shape=jax.ShapeDtypeStruct((SPAN, D), BF...  140 us

profile of v3, /device:TPU:33, one launch (start us, length us, event | category | flops | bytes accessed | tf_op | source)
XLA Modules:
  0.0 142.0 jit_solution(9069016446521307097)
XLA Ops:
  0.0 140.1 %shard_map.109 = bf16[128,2048]{1,0:T(8,128)(2,1)} custom-call(s32[8,128]{1,0:T(8,128)} %bitcast.4, f32[8,128]{1,0:T(8,128)} %bitcast.5, s32[1,2]{1,0:T(1,128)} %seg_len.1, f32[1,2048]{1,0:T(1,128)} %bitcast.3, bf16[128,2048]{1,0:T(8,128)(2,1)} %resid.1, bf16[128,2048]{1,0:T(8,128)(2,1)} %queries.1, bf16[2,128,2048]{2,1,0:T(8,128)(2,1)} %span_kv.1, ...), custom_call_target="tpu_custom_call" | custom-call | tf_op jit(solution)/shard_map/pallas_call | solution.py:515
  140.1 1.9 %copy.13 = bf16[128,2048]{1,0:T(8,128)(2,1)} copy(bf16[128,2048]{1,0:T(8,128)(2,1)} %shard_map.109) | data formatting | bytes 1048576

commit v4 on v3

--- a/solution.py
+++ b/solution.py
@@ -319,7 +319,7 @@
             spot = pl.ds(pl.multiple_of(OZ + ring(x, 2 * n + i, NX) * OX, OX), OX)
             prs[:, :, spot] = got[:, :, i * OX : (i + 1) * OX]
 
-    lax.fori_loop(0, OZ // 256, project_z, 0)
+    lax.fori_loop(0, OZ // 256, project_z, 0, unroll=True)
     for n in range(NX * OX // 256):
         project_x(n)
     c_pr = remote(prs.at[1 - c], pr, sib)
@@ -354,7 +354,7 @@
                 xs[yy, i * CAP : (i + 1) * CAP, cols] = rows[yy * CAP : (yy + 1) * CAP]
             return carry
 
-        lax.fori_loop(0, D // 512, tile, 0)
+        lax.fori_loop(0, D // 512, tile, 0, unroll=True)
 
     def mlp(yy, lo, hi):
         part = slice(lo * CAP, hi * CAP)
@@ -372,7 +372,7 @@
             hb[:count, gate] = (a * (1.0 / (1.0 + jnp.exp(-a))) * b).astype(BF16)
             return carry
 
-        lax.fori_loop(0, FF // 256, up, 0)
+        lax.fori_loop(0, FF // 256, up, 0, unroll=count <= 3 * CAP)
 
         def down(n, carry):
             cols = pl.ds(pl.multiple_of(n * 512, 512), 512)
@@ -381,7 +381,7 @@
             ).astype(BF16)
             return carry
 
-        lax.fori_loop(0, D // 512, down, 0)
+        lax.fori_loop(0, D // 512, down, 0, unroll=True)
 
     def mlps(which, lo, hi):
         lax.fori_loop(which[0], which[1], lambda i, carry: (mlp(ring(y, i, NY), lo, hi), carry)[1], 0)
@@ -430,6 +430,9 @@
             tok[src, :, pieces[j]] = got.astype(BF16)
             send(way, k, j)
 
+    v_y.step(1)
+    share(0, "y")
+    share(1, "y")
     place(z, 0)
     i_x[0].step(1)
     t_z[0].step(1)
@@ -439,19 +442,16 @@
     local[5].wait()
     local[6].wait()
     local[7].wait()
-    v_y.step(1)
-    share(0, "y")
-    share(1, "y")
     t_z[1].step(1)
     place(zs_f[1], 1)
+    u_y.step(1)
+    share(0, "o")
+    share(1, "o")
     place(zs_b[1], 2)
     mlp(y, 0, 3)
     t_z[0].step(2)
     i_x[0].step_f(2)
     share(0, "x")
-    u_y.step(1)
-    share(0, "o")
-    share(1, "o")
     t_z[1].step(2)
     i_x[1].step_f(2)
     share(1, "x")

time: 143 us -> 139 us (0.972)
  Pallas kernels: 140 us -> 136 us
    pallas_call x1, Pallas kernels: 140 us -> 136 us  [shards(): pl.pallas_call(layer_kernel, out_shape=jax.ShapeDtypeStruct((SPAN, D), BF...]
where the time goes in v4:
time: 139 us; the launch traced here: 138 us
  Pallas kernels  136 us (98%)
  local copies, waits for them, and re-layouts  1.88 us (1%)
    pallas_call x1, Pallas kernels, shards(): pl.pallas_call(layer_kernel, out_shape=jax.ShapeDtypeStruct((SPAN, D), BF...  136 us

profile of v4, /device:TPU:33, one launch (start us, length us, event | category | flops | bytes accessed | tf_op | source)
XLA Modules:
  0.0 138.3 jit_solution(11561985607919057481)
XLA Ops:
  0.0 136.4 %shard_map.109 = bf16[128,2048]{1,0:T(8,128)(2,1)} custom-call(s32[8,128]{1,0:T(8,128)} %bitcast.4, f32[8,128]{1,0:T(8,128)} %bitcast.5, s32[1,2]{1,0:T(1,128)} %seg_len.1, f32[1,2048]{1,0:T(1,128)} %bitcast.3, bf16[128,2048]{1,0:T(8,128)(2,1)} %resid.1, bf16[128,2048]{1,0:T(8,128)(2,1)} %queries.1, bf16[2,128,2048]{2,1,0:T(8,128)(2,1)} %span_kv.1, ...), custom_call_target="tpu_custom_call" | custom-call | tf_op jit(solution)/shard_map/pallas_call | solution.py:515
  136.4 1.9 %copy.13 = bf16[128,2048]{1,0:T(8,128)(2,1)} copy(bf16[128,2048]{1,0:T(8,128)(2,1)} %shard_map.109) | data formatting | bytes 1048576

commit v5 on v4

--- a/solution.py
+++ b/solution.py
@@ -372,7 +372,7 @@
             hb[:count, gate] = (a * (1.0 / (1.0 + jnp.exp(-a))) * b).astype(BF16)
             return carry
 
-        lax.fori_loop(0, FF // 256, up, 0, unroll=count <= 3 * CAP)
+        lax.fori_loop(0, FF // 256, up, 0, unroll=True)
 
         def down(n, carry):
             cols = pl.ds(pl.multiple_of(n * 512, 512), 512)
@@ -384,7 +384,7 @@
         lax.fori_loop(0, D // 512, down, 0, unroll=True)
 
     def mlps(which, lo, hi):
-        lax.fori_loop(which[0], which[1], lambda i, carry: (mlp(ring(y, i, NY), lo, hi), carry)[1], 0)
+        lax.fori_loop(which[0], which[1], lambda i, carry: (mlp(ring(y, i, NY), lo, hi), carry)[1], 0, unroll=True)
 
     dims = (((0,), (0,)), ((), ()))
 
@@ -469,9 +469,9 @@
     share(2, "x")
     t_z[1].step(3)
     place(zs_b[3], 5)
-    mlp(y, 3, 6)
     u_y.step_f(2)
     share(2, "o")
+    mlp(y, 3, 6)
     mlp(others[0], 5, 6)
     mlp(others[1], 5, 6)
     have(2)

time: 139 us -> 137 us (0.986)
    pallas_call x1, Pallas kernels: 136 us -> 135 us  [shards(): pl.pallas_call(layer_kernel, out_shape=jax.ShapeDtypeStruct((SPAN, D), BF...]
where the time goes in v5:
time: 137 us; the launch traced here: 136 us
  Pallas kernels  135 us (99%)
  local copies, waits for them, and re-layouts  1.88 us (1%)
    pallas_call x1, Pallas kernels, shards(): pl.pallas_call(layer_kernel, out_shape=jax.ShapeDtypeStruct((SPAN, D), BF...  135 us

profile of v5, /device:TPU:33, one launch (start us, length us, event | category | flops | bytes accessed | tf_op | source)
XLA Modules:
  0.0 136.5 jit_solution(13774750773117744197)
XLA Ops:
  0.0 134.6 %shard_map.109 = bf16[128,2048]{1,0:T(8,128)(2,1)} custom-call(s32[8,128]{1,0:T(8,128)} %bitcast.4, f32[8,128]{1,0:T(8,128)} %bitcast.5, s32[1,2]{1,0:T(1,128)} %seg_len.1, f32[1,2048]{1,0:T(1,128)} %bitcast.3, bf16[128,2048]{1,0:T(8,128)(2,1)} %resid.1, bf16[128,2048]{1,0:T(8,128)(2,1)} %queries.1, bf16[2,128,2048]{2,1,0:T(8,128)(2,1)} %span_kv.1, ...), custom_call_target="tpu_custom_call" | custom-call | tf_op jit(solution)/shard_map/pallas_call | solution.py:515
  134.6 1.9 %copy.13 = bf16[128,2048]{1,0:T(8,128)(2,1)} copy(bf16[128,2048]{1,0:T(8,128)(2,1)} %shard_map.109) | data formatting | bytes 1048576

commit v6 on v5

--- a/solution.py
+++ b/solution.py
@@ -242,7 +242,7 @@
         return carry
 
     def heads(lo, hi):
-        lax.fori_loop(lo, hi, head, 0)
+        lax.fori_loop(lo, hi, head, 0, unroll=True)
 
     i_y.start()
     v_y.start()

time: 137 us -> 137 us (level); the launches traced: 136 us -> 135 us
  Pallas kernels: 135 us -> 133 us
    pallas_call x1, Pallas kernels: 135 us -> 133 us  [shards(): pl.pallas_call(layer_kernel, out_shape=jax.ShapeDtypeStruct((SPAN, D), BF...]
where the time goes in v6:
time: 137 us; the launch traced here: 135 us
  Pallas kernels  133 us (97%)
  local copies, waits for them, and re-layouts  1.88 us (1%)
    pallas_call x1, Pallas kernels, shards(): pl.pallas_call(layer_kernel, out_shape=jax.ShapeDtypeStruct((SPAN, D), BF...  133 us

profile of v6, /device:TPU:33, one launch (start us, length us, event | category | flops | bytes accessed | tf_op | source)
XLA Modules:
  0.0 135.1 jit_solution(6317221855025783472)
XLA Ops:
  0.0 133.2 %shard_map.109 = bf16[128,2048]{1,0:T(8,128)(2,1)} custom-call(s32[8,128]{1,0:T(8,128)} %bitcast.4, f32[8,128]{1,0:T(8,128)} %bitcast.5, s32[1,2]{1,0:T(1,128)} %seg_len.1, f32[1,2048]{1,0:T(1,128)} %bitcast.3, bf16[128,2048]{1,0:T(8,128)(2,1)} %resid.1, bf16[128,2048]{1,0:T(8,128)(2,1)} %queries.1, bf16[2,128,2048]{2,1,0:T(8,128)(2,1)} %span_kv.1, ...), custom_call_target="tpu_custom_call" | custom-call | tf_op jit(solution)/shard_map/pallas_call | solution.py:515
  133.2 1.9 %copy.13 = bf16[128,2048]{1,0:T(8,128)(2,1)} copy(bf16[128,2048]{1,0:T(8,128)(2,1)} %shard_map.109) | data formatting | bytes 1048576
